TPU v7x, 256 devices: a whole 4x4x8 slice. The times are simulated.
256 devices in a mesh: seq: 64 (over y, x_hi, z), head: 4 (over x_lo, core).
Axes of the slice: x: 4 (x_hi: 2, x_lo: 2; x = x_hi * 2 + x_lo), y: 4, z: 8, core: 2. Of those that a mesh axis runs over, the one named last changes fastest.
Arguments:
- queries: bfloat16 [8192, 2048], P('seq', 'head'), may hold values from -15 to 15
- key_heads: bfloat16 [8192, 512], P('seq', 'head'), may hold values from -6 to 6
- value_heads: bfloat16 [8192, 512], P('seq', 'head'), may hold values from -6 to 6
- residual: bfloat16 [8192, 3584], P('seq', 'head'), may hold values from -20 to 20
- out_proj: bfloat16 [2048, 3584], P('head'), may hold values from -0.5 to 0.5
- norm_gain: bfloat16 [3584], P('head'), may hold values from 0.099609375 to 1.8984375
- routes: int32 [8192, 4], P('seq'), may hold values from 0 to 63, all different within a row; in each aligned block of 128 rows (0 to 127, 128 to 255, ...) at most 10 rows name the same one
- combine_weight: float32 [8192, 4], P('seq'), may hold values from 0.05 to 1
- gate_up: bfloat16 [64, 3584, 2, 1280], P('seq', None, None, 'head'), may hold values from -0.09375 to 0.09375
- down_proj: bfloat16 [64, 1280, 3584], P('seq', 'head'), may hold values from -0.15625 to 0.15625
Outputs:
- residual_mid: bfloat16 [8192, 3584], P('seq', 'head')
- expert_out: bfloat16 [8192, 3584], P('seq', 'head')
Inputs may be any that keep to these rules, and one draw needn't show every extreme that they name: `routes`: in the rows of one index of seq (128 positions) no expert is named more than 10 times, and this bound is reached in every draw.
All inputs are finite; a program needn't handle non-finite values.
Results may differ from a plain program's by a relative error of at most 0.03.
Values may be sent and summed in bfloat16 or wider, within the bound.
A program may use at most 128 MiB of HBM per device.

v0:
```python
import math

import jax
import jax.numpy as jnp
from jax import lax
from jax.sharding import PartitionSpec as P

D = 3584
HD = 128
EXPERTS = 64
CAP = 10


epsilon = 1e-06


def body(
    queries,
    key_heads,
    value_heads,
    residual,
    out_proj,
    norm_gain,
    routes,
    combine_weight,
    gate_up,
    down_proj,
):
    token_count = queries.shape[0]
    kv_local = key_heads.shape[1] // HD
    group_size = queries.shape[1] // key_heads.shape[1]
    query_four = queries.reshape(token_count, kv_local, group_size, HD)
    inv_scale = 1.0 / math.sqrt(HD)
    running_max = jnp.full((kv_local, group_size, token_count), -1e30, jnp.float32)
    key_piece = lax.all_gather(key_heads, "seq", axis=0, tiled=True)
    value_piece = lax.all_gather(value_heads, "seq", axis=0, tiled=True)
    piece_rows = key_piece.shape[0]
    key_three = key_piece.reshape(piece_rows, kv_local, HD)
    value_three = value_piece.reshape(piece_rows, kv_local, HD)
    scores = (
        jnp.einsum("tkgd,rkd->kgtr", query_four, key_three, preferred_element_type=jnp.float32)
        * inv_scale
    )
    new_max = jnp.maximum(running_max, jnp.max(scores, axis=3))
    weights = jnp.exp(scores - new_max[..., None])
    new_sum = jnp.sum(weights, axis=3)
    new_acc = jnp.einsum(
        "kgtr,rkd->kgtd",
        weights.astype(jnp.bfloat16),
        value_three,
        preferred_element_type=jnp.float32,
    )
    attended = (
        (new_acc / new_sum[..., None])
        .transpose(2, 0, 1, 3)
        .reshape(token_count, -1)
        .astype(jnp.bfloat16)
    )
    projected = jnp.dot(attended, out_proj, preferred_element_type=jnp.float32)
    summed = lax.psum_scatter(
        projected.astype(jnp.bfloat16), "head", scatter_dimension=1, tiled=True
    ).astype(jnp.float32)
    residual_mid = (residual.astype(jnp.float32) + summed).astype(jnp.bfloat16)
    mid_float = residual_mid.astype(jnp.float32)
    square_total = lax.psum(jnp.sum(mid_float * mid_float, axis=1), "head")
    normed = (
        mid_float * lax.rsqrt(square_total[:, None] / D + epsilon) * norm_gain.astype(jnp.float32)
    ).astype(jnp.bfloat16)
    flat_routes = routes.reshape(-1)
    onehot = (flat_routes[:, None] == jnp.arange(EXPERTS, dtype=jnp.int32)[None, :]).astype(
        jnp.int32
    )
    slot_index = jnp.sum((jnp.cumsum(onehot, axis=0) - onehot) * onehot, axis=1)
    owners = jnp.arange(flat_routes.shape[0], dtype=jnp.int32) // routes.shape[1]
    slot_table = (
        jnp.full((EXPERTS, CAP), token_count, jnp.int32).at[flat_routes, slot_index].set(owners)
    )
    local_experts = gate_up.shape[0]
    gate_up_flat = gate_up.reshape(local_experts, gate_up.shape[1], -1)
    whole_rows = lax.all_gather(normed, "head", axis=1, tiled=True)
    padded = jnp.concatenate(
        [whole_rows, jnp.zeros((1, whole_rows.shape[1]), jnp.bfloat16)], axis=0
    )
    outbound = padded[slot_table]
    received = lax.all_to_all(outbound, "seq", split_axis=0, concat_axis=0, tiled=True)
    slot_width = received.shape[1]
    grouped = received.reshape(-1, local_experts, slot_width, received.shape[2])
    gate_and_up = jnp.einsum(
        "secd,edf->secf", grouped, gate_up_flat, preferred_element_type=jnp.float32
    )
    half_width = gate_and_up.shape[3] // 2
    activated = (jax.nn.silu(gate_and_up[..., :half_width]) * gate_and_up[..., half_width:]).astype(
        jnp.bfloat16
    )
    partial_value = jnp.einsum(
        "secf,efd->secd", activated, down_proj, preferred_element_type=jnp.float32
    )
    reduced = lax.psum_scatter(
        partial_value.astype(jnp.bfloat16), "head", scatter_dimension=3, tiled=True
    )
    returned_raw = lax.all_to_all(
        reduced.reshape(-1, slot_width, reduced.shape[3]),
        "seq",
        split_axis=0,
        concat_axis=0,
        tiled=True,
    )
    picked = (
        returned_raw[flat_routes, slot_index]
        .astype(jnp.float32)
        .reshape(token_count, routes.shape[1], -1)
    )
    expert_out = jnp.sum(combine_weight[:, :, None] * picked, axis=1).astype(jnp.bfloat16)
    return (residual_mid, expert_out)


def solution(mesh):
    placed = (
        P("seq", "head"),
        P("seq", "head"),
        P("seq", "head"),
        P("seq", "head"),
        P("head", None),
        P("head"),
        P("seq", None),
        P("seq", None),
        P("seq", None, None, "head"),
        P("seq", "head", None),
    )
    return jax.shard_map(
        body,
        mesh=mesh,
        in_specs=placed,
        out_specs=(P("seq", "head"), P("seq", "head")),
        check_vma=False,
    )
```

profile of v0, /device:TPU:1, one launch (start us, length us, event | category | flops | bytes accessed | tf_op | source)
XLA Modules:
  0.0 671.4 jit_solution(7373162382854434626)
XLA Ops:
  7.2 0.0 copy-start
  7.2 0.0 all-gather.3.cloned.1.call-start
  7.2 0.7 all-gather.3.cloned.1.call-update
  7.9 0.0 all-gather.5.cloned.1.call-start
  8.0 1.5 copy.29
  9.4 0.0 all-gather.5.cloned.1.call-update
  9.5 0.0 reduce-scatter.7.cloned.1.call-start
  9.5 121.3 %all-gather.3.cloned.1.call-done = bf16[8192,128]{1,0:T(8,128)(2,1)} async-done(((bf16[128,128]{1,0:T(8,128)(2,1)}), bf16[8192,128]{1,0:T(8,128)(2,1)}) %all-gather.3.cloned.1.call-update) | async-done | bytes 2097168 | tf_op jit(solution)/shard_map/all_gather | solution.py:35
  130.8 9.6 %bitcast_reduce_fusion = (f32[4,128]{1,0:T(4,128)S(1)}, f32[8192,128,4]{1,0,2:T(8,128)}) fusion(bf16[8192,128]{1,0:T(8,128)(2,1)} %all-gather.3.cloned.1.call-done, bf16[128,512]{1,0:T(8,128)(2,1)} %param.10), kind=kOutput, calls=%fused_computation.4 | convolution fusion | flops 1082129920 | bytes 19007488 | tf_op jit(solution)/shard_map/tkgd,rkd->kgtr/dot_general | solution.py:41
  140.4 8.5 %fusion.1 = f32[4,128]{1,0:T(4,128)S(1)} fusion(f32[8192,128,4]{1,0,2:T(8,128)} %get-tuple-element.7, f32[4,128]{1,0:T(4,128)S(1)} %broadcast_maximum_fusion), kind=kLoop, calls=%fused_computation.6 | loop fusion | flops 12582400 | bytes 16781312 | tf_op jit(solution)/shard_map/reduce_sum | solution.py:46
  148.9 91.8 %all-gather.5.cloned.1.call-done = bf16[8192,128]{0,1:T(8,128)(2,1)} async-done(((bf16[128,128]{0,1:T(8,128)(2,1)}), bf16[8192,128]{0,1:T(8,128)(2,1)}) %all-gather.5.cloned.1.call-update) | async-done | bytes 2097168 | tf_op jit(solution)/shard_map/all_gather | solution.py:36
  240.7 0.0 copy-start.1
  240.7 9.4 %fusion.21 = bf16[4,128,128]{1,2,0:T(8,128)(2,1)S(1)} fusion(f32[8192,128,4]{1,0,2:T(8,128)} %get-tuple-element.7, f32[4,128]{1,0:T(4,128)S(1)} %broadcast_maximum_fusion, bf16[8192,128]{0,1:T(8,128)(2,1)} %all-gather.5.cloned.1.call-done, f32[4,128]{1,0:T(4,128)S(1)} %fusion.1), kind=kOutput, calls=%fused_computation.22 | convolution fusion | flops 1086455808 | bytes 19009536 | tf_op jit(solution)/shard_map/kgtr,rkd->kgtd/dot_general | solution.py:47
  250.1 0.0 copy-start.4
  250.1 0.0 copy-start.5
  250.1 0.0 copy-done.1
  250.2 0.7 convolution_convert_fusion.1
  250.8 0.0 copy-start.3
  250.8 1.3 copy.44
  252.1 0.0 reduce-scatter.7.cloned.1.call-update
  252.2 0.0 reduce-scatter.9.cloned.1.call-start
  252.2 0.0 copy-done.4
  252.2 0.1 copy.32
  252.3 0.1 eq.29
  252.4 0.1 eq.25
  252.5 0.1 reshape.133
  252.7 0.0 copy-done.5
  252.7 1.2 reduce-window.6
  253.9 0.2 slice_reduce_fusion
  254.2 0.1 fusion.34
  254.3 25.2 %scatter_fusion = s32[64,10]{0,1:T(8,128)S(1)} fusion(s32[64,10]{0,1:T(8,128)S(1)} %broadcast_in_dim.7, s32[512]{0:T(512)S(1)} %bitcast.108, s32[512]{0:T(512)S(1)} %add_select_fusion), kind=kCustom, calls=%fused_computation.2 | custom fusion | bytes 10240 | tf_op jit(solution)/shard_map/scatter | solution.py:76
  279.6 0.1 copy.36
  279.7 0.1 reshape.142
  279.8 0.0 reduce-scatter.7.cloned.1.call-done
  279.8 1.1 copy.45
  280.9 0.0 copy-done.3
  280.9 0.2 fusion.29
  281.1 0.0 copy-start.2
  281.1 8.7 %psum.7 = f32[128]{0:T(128)S(1)} all-reduce(f32[128]{0:T(128)S(1)} %get-tuple-element.4), channel_id=1, replica_groups=mesh['seq'=64,'head'=4] {'head'}, use_global_device_ids=true, to_apply=%region_4.0 | all-reduce | flops 128 | bytes 1024 | tf_op jit(solution)/shard_map/psum | solution.py:65
  289.9 0.1 fusion.31
  290.0 0.0 copy-done.2
  290.0 9.6 %all_gather.11 = bf16[128,3584]{1,0:T(8,128)(2,1)S(1)} all-gather(bf16[128,896]{1,0:T(8,128)(2,1)S(1)} %fusion.31), channel_id=1, replica_groups=mesh['seq'=64,'head'=4] {'head'}, dimensions={1}, use_global_device_ids=true | all-gather | bytes 1146880 | tf_op jit(solution)/shard_map/all_gather | solution.py:80
  299.6 0.1 concatenate.7
  299.7 5.2 gather_fusion
  304.9 7.7 %reshape.141 = bf16[64,10,3584]{2,1,0:T(8,128)(2,1)} reshape(bf16[640,3584]{1,0:T(8,128)(2,1)} %gather_fusion) | data formatting | bytes 9175040 | tf_op jit(solution)/shard_map/gather | solution.py:84
  312.6 171.2 %all_to_all.10 = bf16[64,10,3584]{2,1,0:T(8,128)(2,1)S(1)} all-to-all(bf16[64,10,3584]{2,1,0:T(8,128)(2,1)} %reshape.141), channel_id=1, replica_groups=mesh['seq'=64,'head'=4] {'seq'}, dimensions={0} | all-to-all | bytes 9175040 | tf_op jit(solution)/shard_map/all_to_all | solution.py:85
  483.7 10.0 %fusion.13 = f32[64,1,10,640]{3,0,2,1:T(8,128)S(1)} fusion(bf16[3584,640,1]{0,1,2:T(8,128)(2,1)} %bitcast.114, bf16[64,10,3584]{2,1,0:T(8,128)(2,1)S(1)} %all_to_all.10), kind=kOutput, calls=%fused_computation.20 | convolution fusion | flops 2936012800 | bytes 10813440 | tf_op jit(solution)/shard_map/secd,edf->secf/dot_general | solution.py:88
  493.7 0.0 copy-done
  493.7 4.7 fusion.6
  498.4 16.6 %copy.46 = bf16[64,1,10,3584]{0,2,1,3:T(8,128)(2,1)} copy(bf16[64,1,10,3584]{3,0,2,1:T(8,128)(2,1)} %fusion.6) | data formatting | bytes 9175040
  515.1 17.3 %reshape.168 = bf16[3584,640]{1,0:T(8,128)(2,1)} reshape(bf16[3584,1,10,64]{3,2,1,0:T(8,128)(2,1)} %bitcast.106) | data formatting | bytes 9175040
  532.4 0.0 reduce-scatter.9.cloned.1.call-update
  532.4 48.8 %reduce-scatter.9.cloned.1.call-done = bf16[896,640]{1,0:T(8,128)(2,1)} async-done(((bf16[3584,640]{1,0:T(8,128)(2,1)}), bf16[896,640]{1,0:T(8,128)(2,1)}) %reduce-scatter.9.cloned.1.call-update) | async-done | bytes 1146896
  581.2 5.2 reshape.169
  586.4 0.0 copy-start.6
  586.4 6.8 %copy.39 = bf16[64,10,896]{2,1,0:T(8,128)(2,1)} copy(bf16[64,10,896]{0,1,2:T(8,128)(2,1)} %bitcast.109) | data formatting | bytes 2293760 | tf_op jit(solution)/shard_map/reshape | solution.py:102
  593.2 12.6 %all-to-all-start.1 = ((bf16[64,10,896]{2,1,0:T(8,128)(2,1)}), bf16[64,10,896]{2,1,0:T(8,128)(2,1)}, u32[]{:S(2)}, u32[]{:S(2)}) async-start(bf16[64,10,896]{2,1,0:T(8,128)(2,1)} %copy.39), calls=%async_computation.1 | async-start | bytes 3670016 | tf_op jit(solution)/shard_map/all_to_all | solution.py:101
  605.8 0.0 copy-done.6
  605.8 0.1 copy.31
  605.9 43.6 %all-to-all-done.1 = bf16[64,10,896]{2,1,0:T(8,128)(2,1)} async-done(((bf16[64,10,896]{2,1,0:T(8,128)(2,1)}), bf16[64,10,896]{2,1,0:T(8,128)(2,1)}, u32[]{:S(2)}, u32[]{:S(2)}) %all-to-all-start.1) | async-done | bytes 1146912 | tf_op jit(solution)/shard_map/all_to_all | solution.py:101
  649.5 1.7 copy.40
  651.2 7.5 %gather_fusion.1 = bf16[512,896]{1,0:T(8,128)(2,1)} fusion(bf16[64,10,896]{2,0,1:T(8,128)(2,1)S(1)} %copy.40, s32[512]{0:T(512)S(1)} %bitcast.107), kind=kCustom, calls=%fused_computation.1 | custom fusion | bytes 1839104 | tf_op jit(solution)/shard_map/gather | solution.py:109
  658.8 2.7 reshape.139
  661.5 3.4 multiply_reduce_fusion
  (11 shorter events, 0.1 us)
Async XLA Ops:
  7.2 486.6 %copy-start = (bf16[1,320,3584]{2,1,0:T(8,128)(2,1)S(1)}, bf16[1,320,3584]{2,1,0:T(8,128)(2,1)}, u32[]{:S(2)}) copy-start(bf16[1,320,3584]{2,1,0:T(8,128)(2,1)} %param.19) | copy-start | bytes 6881284
  7.2 123.6 %all-gather.3.cloned.1.call-start = ((), (), s32[]{:S(2)}) async-start(), calls=%async_computation.4 | async-start | bytes 2129920 | tf_op jit(solution)/shard_map/all_gather | solution.py:35
  7.9 232.8 %all-gather.5.cloned.1.call-start = ((), (), s32[]{:S(2)}) async-start(), calls=%async_computation.5 | async-start | bytes 2129920 | tf_op jit(solution)/shard_map/all_gather | solution.py:36
  9.5 270.4 %reduce-scatter.7.cloned.1.call-start = ((), (), s32[]{:S(2)}) async-start(), calls=%async_computation.6 | async-start | bytes 1146880
  240.7 9.4 %copy-start.1 = (bf16[512,3584]{1,0:T(8,128)(2,1)S(1)}, bf16[512,3584]{1,0:T(8,128)(2,1)}, u32[]{:S(2)}) copy-start(bf16[512,3584]{1,0:T(8,128)(2,1)} %param.14) | copy-start | bytes 11010052
  250.1 2.1 copy-start.4
  250.1 2.5 copy-start.5
  250.8 30.1 %copy-start.3 = (bf16[128,896]{1,0:T(8,128)(2,1)S(1)}, bf16[128,896]{1,0:T(8,128)(2,1)}, u32[]{:S(2)}) copy-start(bf16[128,896]{1,0:T(8,128)(2,1)} %param.13) | copy-start | bytes 688132
  252.2 329.1 %reduce-scatter.9.cloned.1.call-start = ((), (), s32[]{:S(2)}) async-start(), calls=%async_computation.7 | async-start | bytes 5734400
  281.1 8.9 %copy-start.2 = (bf16[128,896]{1,0:T(8,128)(2,1)}, bf16[128,896]{1,0:T(8,128)(2,1)S(1)}, u32[]{:S(2)}) copy-start(bf16[128,896]{1,0:T(8,128)(2,1)S(1)} %get-tuple-element.5) | copy-start | bytes 688132
  586.4 19.3 %copy-start.6 = (f32[128,4]{0,1:T(4,128)S(1)}, f32[128,4]{0,1:T(4,128)}, u32[]{:S(2)}) copy-start(f32[128,4]{0,1:T(4,128)} %param.17) | copy-start | bytes 6148
  593.2 56.3 %all-to-all-start.1 = ((bf16[64,10,896]{2,1,0:T(8,128)(2,1)}), bf16[64,10,896]{2,1,0:T(8,128)(2,1)}, u32[]{:S(2)}, u32[]{:S(2)}) async-start(bf16[64,10,896]{2,1,0:T(8,128)(2,1)} %copy.39), calls=%async_computation.1 | async-start | bytes 3670016 | tf_op jit(solution)/shard_map/all_to_all | solution.py:101
Sparse Core Ops, SparseCore 0:
  11.6 119.1 all-gather.2
  134.8 105.8 all-gather.4
  252.3 22.2 reduce-scatter.6
  532.5 48.6 reduce-scatter.8
where the time goes:
time: 675 us; the launch traced here: 671 us
  waiting for transfers between devices  306 us (45%)
  blocking collectives  190 us (28%)
  local copies, waits for them, and re-layouts  101 us (15%)
  matrix products  34.4 us (5%)
  between operations  14 us (2%)
  other arithmetic  13.6 us (2%)
  starting transfers between devices  12.7 us (2%)
    all_to_all x1, blocking collectives, body(): lax.all_to_all(outbound, 'seq', split_axis=0, concat_axis=0, tiled=True)  171 us
    all_gather x1, waiting for transfers between devices, body(): key_piece = lax.all_gather(key_heads, 'seq', axis=0, tiled=True)  121 us
    all_gather x1, waiting for transfers between devices, body(): value_piece = lax.all_gather(value_heads, 'seq', axis=0, tiled=True)  91.8 us
    unnamed x6, waiting for transfers between devices  49.6 us
    all_to_all x1, waiting for transfers between devices, body(): lax.all_to_all(reduced.reshape(-1, slot_width, reduced.shape[3]), 'seq',...  43.6 us
    unnamed x22, local copies, waits for them, and re-layouts  43.3 us
    scatter x1, local copies, waits for them, and re-layouts, body(): jnp.full((EXPERTS, CAP), token_count, jnp.int32).at[flat_routes, slot_index]  25.2 us
  transfers between devices with their start and end apart: 5, of which 4 were waited for; matrix products, arithmetic and copies ran while one was open for 7% of the time, Pallas kernels for 0%

commit v1 on v0

v1 whole, which is shorter than its diff:
```python
import math

import jax
import jax.numpy as jnp
from jax import lax
from jax.experimental import pallas as pl
from jax.experimental.pallas import tpu as pltpu
from jax.sharding import PartitionSpec as P

D = 3584
HD = 128
TOK = 128
QUARTER = 896
HALF = 1792
HID = 320
ROWS_A = 80
SLOT_ROWS = 144
GROUP = 8
GROUPS = 4
GROUP_ROWS = 80
EPSILON = 1e-06
SCALE2 = math.log2(math.e) / math.sqrt(HD)
MESH = pl.DeviceIdType.MESH
F32 = jnp.float32
BF16 = jnp.bfloat16


def dot(a, b):
    return jnp.dot(a, b, preferred_element_type=F32)


def dot_nt(a, b):
    return lax.dot_general(a, b, (((1,), (1,)), ((), ())), preferred_element_type=F32)


def iota(shape, dim):
    return lax.broadcasted_iota(jnp.int32, shape, dim)


def kernel(
    q_ref,
    k_ref,
    v_ref,
    residual_ref,
    out_proj_ref,
    gain_ref,
    routes_ref,
    weight_ref,
    gate_up_ref,
    down_ref,
    mid_ref,
    out_ref,
    kv,
    qr,
    acc,
    row_max,
    part_send,
    part_recv,
    stat_send,
    stat_recv,
    att,
    wo,
    rs_send,
    rs_recv,
    gains,
    mid_half,
    squares,
    wc,
    onehot,
    perm,
    ymat,
    send_buf,
    xbuf,
    xmat,
    gu,
    wd,
    po_send,
    po_recv,
    po_own,
    ret_send,
    ret,
    rmat,
    comb_send,
    comb_recv,
    ra,
    rb,
    rd,
    rp,
    rpo,
    spo,
    rr,
    sa,
    sb,
    sd,
    sp,
    sr,
    misc_send,
    misc_recv,
    weight_send,
    weight_recv,
    weight_local,
):
    seq, head = lax.axis_index("seq"), lax.axis_index("head")
    y, z = lax.div(seq, 16), lax.rem(seq, 8)
    xh = lax.rem(lax.div(seq, 8), 2)
    xl, core = lax.div(head, 2), lax.rem(head, 2)
    other = 1 - core
    z_even, y_even, core_zero = lax.rem(z, 2) == 0, lax.rem(y, 2) == 0, core == 0
    my_kv = z * 4 + y
    my_j = y * 8 + z
    far_h, far_l = (xh + core) % 2, (xl + core) % 2
    half_in = far_l

    def dev(y_, xh_, z_, xl_, core_):
        return {"seq": (y_ * 2 + xh_) * 8 + z_, "head": xl_ * 2 + core_}

    partner = dev(y, xh, z, xl, other)
    pair = dev(y, xh, z, 1 - xl, core)
    diagonal = dev(y, xh, z, 1 - xl, other)
    twin = dev(y, 1 - xh, z, xl, core)

    def wrap(a, n):
        return lax.rem(a + n, n)

    yp, ym, y2 = wrap(y + 1, 4), wrap(y - 1, 4), wrap(y + 2, 4)
    zp, zm = wrap(z + 1, 8), wrap(z - 1, 8)

    def far(j):
        return dev(lax.div(j, 8), far_h, lax.rem(j, 8), far_l, core)

    barrier = pltpu.get_barrier_semaphore()

    def greet(device):
        pl.semaphore_signal(barrier, inc=1, device_id=device, device_id_type=MESH)

    for device in (
        dev(yp, xh, z, xl, core),
        dev(ym, xh, z, xl, core),
        dev(y, xh, zp, xl, core),
        dev(y, xh, zm, xl, core),
        twin,
        partner,
        pair,
        diagonal,
    ):
        greet(device)

    def greet_far(i, carry):
        greet(far(lax.rem(my_j + i, 32)))
        return carry

    lax.fori_loop(1, 32, greet_far, 0)

    @pl.when(core == 1)
    def _():
        greet(far(my_j))

    for j in range(4):
        qr[j * TOK : (j + 1) * TOK, :] = q_ref[:, j * HD : (j + 1) * HD]
    kv[:, :, 256:384] = jnp.ones((32, TOK, HD), BF16)
    kv[my_kv, :, 0:128] = k_ref[...]
    kv[my_kv, :, 128:256] = v_ref[...]
    gains[core, :, :] = jnp.broadcast_to(gain_ref[...].astype(F32), (8, QUARTER))
    pl.semaphore_wait(barrier, 39 + core)

    def rcopy(src, dst, send, recv, device):
        return pltpu.make_async_remote_copy(
            src_ref=src,
            dst_ref=dst,
            send_sem=send,
            recv_sem=recv,
            device_id=device,
            device_id_type=MESH,
        )

    def part_a(b):
        return kv.at[b, pl.ds(0, ROWS_A), pl.ds(0, 256)]

    def part_b(b):
        return kv.at[b, pl.ds(ROWS_A, TOK - ROWS_A), pl.ds(0, 256)]

    def send_a(zb, yb, y_, z_):
        b = zb * 4 + yb
        rcopy(part_a(b), part_a(b), sa, ra.at[b], dev(y_, xh, z_, xl, core)).start()

    def send_b(zb, yb, y_, z_):
        b = zb * 4 + yb
        rcopy(part_b(b), part_b(b), sb, rb.at[b], dev(y_, xh, z_, xl, core)).start()

    def wait_a(zb, yb):
        b = zb * 4 + yb
        pltpu.make_async_copy(part_a(b), part_a(b), ra.at[b]).wait()

    def wait_b(zb, yb):
        b = zb * 4 + yb
        pltpu.make_async_copy(part_b(b), part_b(b), rb.at[b]).wait()

    send_a(z, y, y, zp)
    send_a(z, y, y, zm)
    send_b(z, y, yp, z)
    send_b(z, y, ym, z)
    send_a(z, y, yp, z)
    send_a(z, y, ym, z)
    send_b(z, y, y, zp)
    send_b(z, y, y, zm)
    q_copy = rcopy(
        qr.at[pl.ds(0, 512)], qr.at[pl.ds(512, 512)], misc_send.at[0], misc_recv.at[0], twin
    )
    q_copy.start()
    gain_copy = rcopy(gains.at[core], gains.at[core], misc_send.at[1], misc_recv.at[1], partner)
    gain_copy.start()

    wo_copies = []
    for hf in range(2):
        mine = pl.ds(pl.multiple_of((hf * 2 + core) * QUARTER, 128), QUARTER)
        theirs = pl.ds(pl.multiple_of((hf * 2 + other) * QUARTER, 128), QUARTER)
        wo_copies.append(
            rcopy(
                out_proj_ref.at[:, theirs],
                wo.at[core, hf],
                weight_send.at[hf],
                weight_recv.at[hf],
                partner,
            )
        )
        wo_copies[-1].start()
        wo_copies.append(
            pltpu.make_async_copy(out_proj_ref.at[:, mine], wo.at[core, hf], weight_local.at[hf])
        )
    for copy in wo_copies[1::2]:
        copy.start()
    ffn_copies = []
    for n, (src, dst) in enumerate(((gate_up_ref, gu), (down_ref, wd))):
        remote = rcopy(
            src, dst.at[core], weight_send.at[2 + n], weight_recv.at[2 + n], partner
        )
        local = pltpu.make_async_copy(src, dst.at[core], weight_local.at[2 + n])
        remote.start()
        local.start()
        ffn_copies += [remote, local]

    acc[...] = jnp.zeros((1024, 256), F32)
    row_max[...] = jnp.full((1024, HD), -1e30, F32)

    lane = iota((1, 384), 1)
    main = lane < 256
    extra = lane - 256
    j_row = jnp.where(main, lax.shift_right_logical(lane, 3), lax.shift_right_logical(jnp.maximum(extra, 0), 1))
    s_row = jnp.where(main, lane & 7, 8 + (extra & 1))
    e_row = lax.shift_right_logical(j_row, 3) * 16 + far_h * 8 + (j_row & 7)
    e_row = jnp.where(j_row < 32, e_row, -1)
    named = jnp.zeros((TOK, 384), F32)
    weight = jnp.zeros((TOK, 384), F32)
    for k in range(4):
        same = routes_ref[:, k : k + 1] == e_row
        named = jnp.where(same, 1.0, named)
        weight = jnp.where(same, weight_ref[:, k : k + 1], weight)
    earlier = jnp.where(iota((TOK, TOK), 1) < iota((TOK, TOK), 0), 1.0, 0.0).astype(BF16)
    count = dot(earlier, named.astype(BF16))
    taken = jnp.where(count == s_row.astype(F32), named, 0.0)
    weight = weight * taken
    high = weight.astype(BF16)
    wc[0] = high
    wc[1] = (weight - high.astype(F32)).astype(BF16)
    onehot[...] = taken.T
    for which in range(2):
        o, i = iota((256, 256), which), iota((256, 256), 1 - which)
        rem = o & 31
        source = lax.shift_right_logical(rem, 1) * 16 + lax.shift_right_logical(o, 5) * 2 + (rem & 1)
        perm[which] = jnp.where((source == i) & (rem < 28), 1.0, 0.0).astype(BF16)
    rmat[...] = jnp.zeros((384, HALF), BF16)

    eye = iota((TOK, TOK), 0) == iota((TOK, TOK), 1)

    def to_row(column):
        return jnp.sum(jnp.where(eye, column, 0.0), axis=0, keepdims=True)

    def to_column(row):
        return jnp.sum(jnp.where(eye, row, 0.0), axis=1, keepdims=True)

    def flash(zb, first, count):
        block = kv[pl.ds(zb * 4, 4)]
        keys = block[:, :, 0:128].reshape(512, HD)
        values = block[:, :, 128:384].reshape(512, 256)

        def tile(t, carry):
            rows = pl.ds(pl.multiple_of(first + t * 256, 256), 256)
            scores = dot_nt(qr[rows, :], keys)
            old = row_max[rows, :]
            new = jnp.maximum(old, jnp.max(scores, axis=1, keepdims=True))
            p = jnp.exp2((scores - new[:, 0:1]) * SCALE2).astype(BF16)
            fade = jnp.exp2((old - new) * SCALE2)
            add = dot(p, values)
            acc[rows, 0:128] = acc[rows, 0:128] * fade + add[:, 0:128]
            acc[rows, 128:256] = acc[rows, 128:256] * fade + add[:, 128:256]
            row_max[rows, :] = new
            return carry

        lax.fori_loop(0, count // 256, tile, 0)

    def y_stage(zb):
        even = lax.rem(zb, 2) == 0
        wait_a(zb, ym)

        @pl.when(even)
        def _():
            send_a(zb, ym, yp, z)

        wait_a(zb, yp)

        @pl.when(jnp.logical_not(even))
        def _():
            send_a(zb, yp, ym, z)

    for yb, forward, to in ((ym, z_even, yp), (yp, jnp.logical_not(z_even), ym)):
        wait_b(z, yb)
        send_b(z, yb, y, zp)
        send_b(z, yb, y, zm)

        @pl.when(forward)
        def _():
            send_b(z, yb, to, z)

    y_stage(z)
    wait_b(z, y2)
    send_b(z, y2, y, zp)
    send_b(z, y2, y, zm)

    def z_stage(d):
        for zb, to, parity in ((wrap(z - d, 8), zp, 0), (wrap(z + d, 8), zm, 1)):
            wait_a(zb, y)
            goes = (d < 3) | ((d == 3) & (lax.rem(y, 2) == parity))

            @pl.when(goes)
            def _():
                send_a(zb, y, y, to)

            send_a(zb, y, yp, z)
            send_a(zb, y, ym, z)

            def each(yb, carry):
                wait_b(zb, yb)

                @pl.when((d < 3) | ((d == 3) & (lax.rem(yb, 2) == parity)))
                def _():
                    send_b(zb, yb, y, to)

                return carry

            lax.fori_loop(0, 4, each, 0)

    def step(d, carry):
        z_stage(d)

        @pl.when(d == 1)
        def _():
            q_copy.wait_recv()
            wait_a(z, y2)
            flash(z, 0, 1024)

        @pl.when(d > 1)
        def _():
            for zb in (wrap(z - d + 1, 8), wrap(z + d - 1, 8)):
                wait_a(zb, y2)
                flash(zb, 0, 1024)

        y_stage(wrap(z - d, 8))
        y_stage(wrap(z + d, 8))
        return carry

    lax.fori_loop(1, 4, step, 0)
    zf = wrap(z + 4, 8)
    wait_a(zf, y)
    send_a(zf, y, yp, z)
    send_a(zf, y, ym, z)
    for zb in (wrap(z - 3, 8), wrap(z + 3, 8)):
        wait_a(zb, y2)
        flash(zb, 0, 1024)
    y_stage(zf)
    wait_a(zf, y2)
    for yb in range(4):
        wait_b(zf, yb)

    flash(zf, 512, 512)
    for j in range(4):
        rows = pl.ds(512 + j * TOK, TOK)
        total = acc[rows, 128:256]
        part_send[j * TOK : (j + 1) * TOK, :] = (acc[rows, 0:128] / total).astype(BF16)
        stat_send[j : j + 1, :] = to_row(row_max[rows, :] * SCALE2 + jnp.log2(total))
    stat_send[4:8, :] = jnp.zeros((4, TOK), F32)
    part_copy = rcopy(part_send, part_recv, misc_send.at[2], misc_recv.at[2], twin)
    stat_copy = rcopy(stat_send, stat_recv, misc_send.at[3], misc_recv.at[3], twin)
    part_copy.start()
    stat_copy.start()
    flash(zf, 0, 512)
    part_copy.wait_recv()
    stat_copy.wait_recv()
    for j in range(4):
        rows = slice(j * TOK, (j + 1) * TOK)
        total = acc[rows, 128:256]
        own = acc[rows, 0:128] / total
        own_stat = row_max[rows, :] * SCALE2 + jnp.log2(total)
        their_stat = to_column(stat_recv[j : j + 1, :])
        own_share = 1.0 / (1.0 + jnp.exp2(their_stat - own_stat))
        their_share = 1.0 / (1.0 + jnp.exp2(own_stat - their_stat))
        att[core, :, rows] = (
            own * own_share + part_recv[rows, :].astype(F32) * their_share
        ).astype(BF16)
    att_copy = rcopy(att.at[core], att.at[core], misc_send.at[4], misc_recv.at[4], partner)
    att_copy.start()
    for copy in wo_copies[0::2]:
        copy.wait_recv()
    for copy in wo_copies[1::2]:
        copy.wait()
    gain_copy.wait_recv()
    att_copy.wait_recv()

    def project(hf):
        return dot(att[0], wo[0, hf]) + dot(att[1], wo[1, hf])

    rs_send[...] = project(1 - xl).astype(BF16)
    rs_copy = rcopy(rs_send, rs_recv, misc_send.at[5], misc_recv.at[5], pair)
    rs_copy.start()
    own = project(xl) + residual_ref[...].astype(F32)
    rs_copy.wait_recv()
    middle = (own + rs_recv[...].astype(F32)).astype(BF16)
    mid_half[core, :, :] = middle
    mid_copy = rcopy(
        mid_half.at[core], mid_half.at[core], misc_send.at[6], misc_recv.at[6], partner
    )
    mid_copy.start()
    mid_ref[...] = middle
    mid_float = middle.astype(F32)
    squares[head] = jnp.broadcast_to(
        to_row(jnp.sum(mid_float * mid_float, axis=1, keepdims=True)), (8, TOK)
    )
    square_copies = [
        rcopy(squares.at[head], squares.at[head], misc_send.at[7 + n], misc_recv.at[7 + n], device)
        for n, device in enumerate((partner, pair, diagonal))
    ]
    for copy in square_copies:
        copy.start()
    mid_copy.wait_recv()
    hot = onehot[...]
    hot16 = hot.astype(BF16)
    for c in range(2):
        ymat[:, c * QUARTER : (c + 1) * QUARTER] = dot(hot16, mid_half[c])
    for copy in square_copies:
        copy.wait_recv()
    total = squares[0, 0:1] + squares[1, 0:1] + squares[2, 0:1] + squares[3, 0:1]
    inverse = lax.rsqrt(total / D + EPSILON)
    row_scale = jnp.sum(hot * inverse, axis=1, keepdims=True)

    def lane_block(c):
        return slice(c * 128, (c + 1) * 128)

    def scaled(rows, c):
        q, inner = c // 7, c % 7
        return ymat[rows, lane_block(c)] * row_scale[rows] * gains[q, 0:1, lane_block(inner)]

    for c in range(0, 14, 2):
        both = [scaled(slice(0, 256), c + n).reshape(32, 8, 128) for n in range(2)]
        send_buf[:, c * 8 : c * 8 + 16, :] = jnp.concatenate(both, axis=1).astype(BF16)
    for g in range(4):
        rows = slice(256 + 16 * g, 272 + 16 * g)
        stack = jnp.concatenate(
            [scaled(rows, c).astype(BF16) for c in range(14)] + [jnp.zeros((32, 128), BF16)], axis=0
        )
        send_buf[8 * g : 8 * g + 8, 112:144, :] = (
            dot(perm[0], stack).reshape(8, 32, 128).astype(BF16)
        )

    def exchange(buffer, place, send, recv, first, count):
        def one(i, carry):
            j = lax.rem(my_j + i, 32)
            rcopy(buffer.at[j], place(), send, recv.at[my_j], far(j)).start()
            return carry

        lax.fori_loop(first, count, one, 0)

    def landing():
        return xbuf.at[xl, my_j]

    @pl.when(core_zero)
    def _():
        pltpu.make_async_copy(send_buf.at[my_j], xbuf.at[xl, my_j], rd.at[my_j]).start()

    @pl.when(core == 1)
    def _():
        rcopy(send_buf.at[my_j], landing(), sd, rd.at[my_j], far(my_j)).start()

    exchange(send_buf, landing, sd, rd, 1, 32)

    for copy in ffn_copies[0::2]:
        copy.wait_recv()
    for copy in ffn_copies[1::2]:
        copy.wait()

    def source(i):
        return wrap(my_j - i, 32)

    def forward(g):
        def one(n, carry):
            s = source(g * GROUP + n)
            block = xbuf.at[half_in, s]
            pltpu.make_async_copy(block, block, rd.at[s]).wait()
            rcopy(block, block, sp, rp.at[s], pair).start()
            return carry

        lax.fori_loop(0, GROUP, one, 0)

    def gather_rows(g):
        def await_pair(n, carry):
            s = source(g * GROUP + n)
            block = xbuf.at[1 - half_in, s]
            pltpu.make_async_copy(block, block, rp.at[s]).wait()
            return carry

        lax.fori_loop(0, GROUP, await_pair, 0)
        for half in range(2):
            for p in range(GROUP // 2):
                both = [
                    xbuf[half, source(g * GROUP + 2 * p + n), 0:112, :]
                    .astype(F32)
                    .reshape(14, 8, 128)
                    for n in range(2)
                ]
                rows = jnp.concatenate(both, axis=1).astype(BF16)
                for c in range(14):
                    xmat[16 * p : 16 * p + 16, lane_block(half * 14 + c)] = rows[c]
            stack = jnp.concatenate(
                [xbuf[half, source(g * GROUP + n), 112:144, :] for n in range(GROUP)], axis=0
            )
            rows = dot(perm[1], stack).astype(BF16)
            for c in range(14):
                xmat[64:80, lane_block(half * 14 + c)] = rows[16 * c : 16 * c + 16]

    def experts(g):
        x = xmat[...]
        parts = []
        for c in range(2):
            hidden = dot(x, gu[c])
            gate, up = hidden[:, :HID], hidden[:, HID:]
            parts.append((gate / (1.0 + jnp.exp(-gate)) * up).astype(BF16))

        def result(half, n):
            columns = pl.ds(pl.multiple_of(half * HALF + n * QUARTER, 128), QUARTER)
            return dot(parts[0], wd[0, :, columns]) + dot(parts[1], wd[1, :, columns])

        for n in range(2):
            po_send[g, :, n * QUARTER : (n + 1) * QUARTER] = result(1 - half_in, n).astype(BF16)
        rcopy(po_send.at[g], po_recv.at[g], spo.at[g], rpo.at[g], pair).start()
        for n in range(2):
            po_own[g, :, n * QUARTER : (n + 1) * QUARTER] = result(half_in, n)

    def give_back(g):
        pltpu.make_async_copy(po_recv.at[g], po_recv.at[g], rpo.at[g]).wait()
        first = pl.multiple_of(g * GROUP, GROUP)

        def summed(rows, c):
            return po_own[g, rows, lane_block(c)] + po_recv[g, rows, lane_block(c)].astype(F32)

        for c in range(0, 14, 2):
            both = [summed(slice(0, 64), c + n).reshape(8, 8, 128) for n in range(2)]
            ret_send[pl.ds(first, 8), c * 8 : c * 8 + 16, :] = jnp.concatenate(both, axis=1).astype(
                BF16
            )
        stack = jnp.concatenate(
            [summed(slice(64, 80), c).astype(BF16) for c in range(14)]
            + [jnp.zeros((32, 128), BF16)],
            axis=0,
        )
        ret_send[pl.ds(first, 8), 112:144, :] = dot(perm[0], stack).reshape(8, 32, 128).astype(BF16)

        def one(n, carry):
            i = g * GROUP + n
            s = source(i)

            @pl.when(core_zero & (i == 0))
            def _():
                pltpu.make_async_copy(ret_send.at[i], ret.at[my_j], rr.at[my_j]).start()

            @pl.when(jnp.logical_not(core_zero & (i == 0)))
            def _():
                rcopy(ret_send.at[i], ret.at[my_j], sr, rr.at[my_j], far(s)).start()

            return carry

        lax.fori_loop(0, GROUP, one, 0)

    forward(0)

    def turn(g, carry):
        @pl.when(g < GROUPS - 1)
        def _():
            forward(g + 1)

        gather_rows(g)
        experts(g)

        @pl.when(g > 0)
        def _():
            give_back(g - 1)

        return carry

    lax.fori_loop(0, GROUPS, turn, 0)
    give_back(GROUPS - 1)

    def await_return(i, carry):
        j = lax.rem(my_j + i, 32)
        pltpu.make_async_copy(ret.at[j], ret.at[j], rr.at[j]).wait()
        return carry

    lax.fori_loop(0, 32, await_return, 0)
    for c in range(0, 14, 2):
        both = ret[:, c * 8 : c * 8 + 16, :].astype(F32)
        for n in range(2):
            rmat[0:256, lane_block(c + n)] = both[:, 8 * n : 8 * n + 8].reshape(256, 128).astype(BF16)
    for g in range(4):
        stack = ret[8 * g : 8 * g + 8, 112:144, :].reshape(256, 128)
        rows = dot(perm[1], stack).astype(BF16)
        for c in range(14):
            rmat[256 + 16 * g : 272 + 16 * g, lane_block(c)] = rows[16 * c : 16 * c + 16]

    def combined(which):
        columns = pl.ds(pl.multiple_of(which * QUARTER, 128), QUARTER)
        rows = rmat[:, columns]
        return dot(wc[0], rows) + dot(wc[1], rows)

    comb_send[...] = combined(other).astype(BF16)
    comb_copy = rcopy(comb_send, comb_recv, misc_send.at[10], misc_recv.at[10], partner)
    comb_copy.start()
    own = combined(core)
    comb_copy.wait_recv()
    out_ref[...] = (own + comb_recv[...].astype(F32)).astype(BF16)

    for copy in (
        [q_copy, gain_copy, part_copy, stat_copy, att_copy, rs_copy, mid_copy, comb_copy]
        + square_copies
        + wo_copies[0::2]
        + ffn_copies[0::2]
    ):
        copy.wait_send()
    for g in range(GROUPS):
        pltpu.make_async_copy(po_send.at[g], po_send.at[g], spo.at[g]).wait()

    def drain(ref, sem):
        pltpu.make_async_copy(ref, ref, sem).wait()

    drain(kv.at[pl.ds(0, 31), pl.ds(0, ROWS_A), pl.ds(0, 256)], sa)
    drain(kv.at[pl.ds(0, 31), pl.ds(ROWS_A, TOK - ROWS_A), pl.ds(0, 256)], sb)
    drain(xbuf.at[0], sp)
    for sem in (sd, sr):

        @pl.when(core_zero)
        def _():
            drain(send_buf.at[pl.ds(0, 31)], sem)

        @pl.when(core == 1)
        def _():
            drain(send_buf, sem)


def body(
    queries,
    key_heads,
    value_heads,
    residual,
    out_proj,
    norm_gain,
    routes,
    combine_weight,
    gate_up,
    down_proj,
):
    vmem = pl.BlockSpec(memory_space=pltpu.VMEM)
    hbm = pl.BlockSpec(memory_space=pl.ANY)
    dma = pltpu.SemaphoreType.DMA
    return pl.pallas_call(
        kernel,
        out_shape=(
            jax.ShapeDtypeStruct((TOK, QUARTER), BF16),
            jax.ShapeDtypeStruct((TOK, QUARTER), BF16),
        ),
        in_specs=[vmem, vmem, vmem, vmem, hbm, vmem, vmem, vmem, hbm, hbm],
        out_specs=(vmem, vmem),
        scratch_shapes=[
            pltpu.VMEM((32, TOK, 384), BF16),
            pltpu.VMEM((1024, HD), BF16),
            pltpu.VMEM((1024, 256), F32),
            pltpu.VMEM((1024, HD), F32),
            pltpu.VMEM((512, HD), BF16),
            pltpu.VMEM((512, HD), BF16),
            pltpu.VMEM((8, TOK), F32),
            pltpu.VMEM((8, TOK), F32),
            pltpu.VMEM((2, TOK, 512), BF16),
            pltpu.VMEM((2, 2, 512, QUARTER), BF16),
            pltpu.VMEM((TOK, QUARTER), BF16),
            pltpu.VMEM((TOK, QUARTER), BF16),
            pltpu.VMEM((2, 8, QUARTER), F32),
            pltpu.VMEM((2, TOK, QUARTER), BF16),
            pltpu.VMEM((4, 8, TOK), F32),
            pltpu.VMEM((2, TOK, 384), BF16),
            pltpu.VMEM((384, TOK), F32),
            pltpu.VMEM((2, 256, 256), BF16),
            pltpu.VMEM((384, HALF), F32),
            pltpu.VMEM((32, SLOT_ROWS, 128), BF16),
            pltpu.VMEM((2, 32, SLOT_ROWS, 128), BF16),
            pltpu.VMEM((GROUP_ROWS, D), BF16),
            pltpu.VMEM((2, D, 2 * HID), BF16),
            pltpu.VMEM((2, HID, D), BF16),
            pltpu.VMEM((GROUPS, GROUP_ROWS, HALF), BF16),
            pltpu.VMEM((GROUPS, GROUP_ROWS, HALF), BF16),
            pltpu.VMEM((GROUPS, GROUP_ROWS, HALF), F32),
            pltpu.VMEM((32, SLOT_ROWS, 128), BF16),
            pltpu.VMEM((32, SLOT_ROWS, 128), BF16),
            pltpu.VMEM((384, HALF), BF16),
            pltpu.VMEM((TOK, QUARTER), BF16),
            pltpu.VMEM((TOK, QUARTER), BF16),
            dma((32,)),
            dma((32,)),
            dma((32,)),
            dma((32,)),
            dma((GROUPS,)),
            dma((GROUPS,)),
            dma((32,)),
            dma,
            dma,
            dma,
            dma,
            dma,
            dma((11,)),
            dma((11,)),
            dma((4,)),
            dma((4,)),
            dma((4,)),
        ],
        compiler_params=pltpu.CompilerParams(
            collective_id=0,
            has_side_effects=True,
            vmem_limit_bytes=58 * 1024 * 1024,
        ),
        cost_estimate=pl.CostEstimate(
            flops=8_000_000_000, bytes_accessed=20_000_000, transcendentals=5_000_000
        ),
    )(
        queries,
        key_heads,
        value_heads,
        residual,
        out_proj,
        norm_gain.reshape(1, QUARTER),
        routes,
        combine_weight,
        gate_up.reshape(D, 2 * HID),
        down_proj.reshape(HID, D),
    )


def solution(mesh):
    placed = (
        P("seq", "head"),
        P("seq", "head"),
        P("seq", "head"),
        P("seq", "head"),
        P("head", None),
        P("head"),
        P("seq", None),
        P("seq", None),
        P("seq", None, None, "head"),
        P("seq", "head", None),
    )
    return jax.shard_map(
        body,
        mesh=mesh,
        in_specs=placed,
        out_specs=(P("seq", "head"), P("seq", "head")),
        check_vma=False,
    )
```

time: 675 us -> 163 us (0.24)
  waiting for transfers between devices: 306 us -> 0 us
  blocking collectives: 190 us -> 0 us
  Pallas kernels: 0 us -> 147 us
  local copies, waits for them, and re-layouts: 101 us -> 14.6 us
  matrix products: 34.4 us -> 0 us
  other arithmetic: 13.6 us -> 0 us
  between operations: 14 us -> 0.64 us
  starting transfers between devices: 12.7 us -> 0 us
    all_gather x2 -> x0, waiting for transfers between devices: 213 us -> none  [the longest x1 121 us: body(): key_piece = lax.all_gather(key_heads, 'seq', axis=0, tiled=True)]
    all_to_all x1 -> x0, blocking collectives: 171 us -> none  [body(): lax.all_to_all(outbound, 'seq', split_axis=0, concat_axis=0, tiled=True)]
    pallas_call x0 -> x1, Pallas kernels: none -> 147 us  [body(): pl.pallas_call(kernel, out_shape=(jax.ShapeDtypeStruct((TOK, QUARTER), BF...]
    unnamed x6 -> x0, waiting for transfers between devices: 49.6 us -> none
    all_to_all x1 -> x0, waiting for transfers between devices: 43.6 us -> none  [body(): lax.all_to_all(reduced.reshape(-1, slot_width, reduced.shape[3]), 'seq',...]
    unnamed x22 -> x4, local copies, waits for them, and re-layouts: 43.3 us -> 6.12 us
    dot_general x5 -> x0, matrix products: 34.4 us -> none  [the longest x1 9.97 us: body(): jnp.einsum('secd,edf->secf', grouped, gate_up_flat, preferred_element_typ...]
    scatter x1 -> x0, local copies, waits for them, and re-layouts: 25.2 us -> none  [body(): jnp.full((EXPERTS, CAP), token_count, jnp.int32).at[flat_routes, slot_index]]
  transfers between devices with their start and end apart: 5 -> 0, of which waited for: 4 -> 0; matrix products, arithmetic and copies ran while one was open for 7% -> 0% of each run, Pallas kernels for 0% -> 0%
where the time goes in v1:
time: 163 us; the launch traced here: 162 us
  Pallas kernels  147 us (90%)
  local copies, waits for them, and re-layouts  14.6 us (9%)
    pallas_call x1, Pallas kernels, body(): pl.pallas_call(kernel, out_shape=(jax.ShapeDtypeStruct((TOK, QUARTER), BF...  147 us
    reshape x1, local copies, waits for them, and re-layouts, body(): gate_up.reshape(D, 2 * HID)  7.22 us
    unnamed x4, local copies, waits for them, and re-layouts  6.12 us

profile of v1, /device:TPU:1, one launch (start us, length us, event | category | flops | bytes accessed | tf_op | source)
XLA Modules:
  0.0 162.2 jit_solution(10607233814194131771)
XLA Ops:
  0.6 1.3 reshape.13.gain_ref
  1.9 1.4 copy.15.routes_ref
  3.3 1.4 copy.16.weight_ref
  4.7 7.2 %copy.17.gate_up_ref = bf16[3584,640]{1,0:T(8,128)(2,1)} copy(bf16[3584,640]{0,1:T(8,128)(2,1)} %bitcast.2) | data formatting | bytes 9175040 | tf_op jit(solution)/shard_map/reshape | solution.py:756
  11.9 146.9 %shard_map.113 = (bf16[128,896]{1,0:T(8,128)(2,1)}, bf16[128,896]{1,0:T(8,128)(2,1)}) custom-call(bf16[128,512]{1,0:T(8,128)(2,1)} %q_ref.1, bf16[128,128]{1,0:T(8,128)(2,1)} %k_ref.1, bf16[128,128]{1,0:T(8,128)(2,1)} %v_ref.1, bf16[128,896]{1,0:T(8,128)(2,1)} %residual_ref.1, bf16[512,3584]{1,0:T(8,128)(2,1)} %out_proj_ref.1, ...), custom_call_target="tpu_custom_call" | custom-call | flops 8000000000 | bytes 20000000 | tf_op jit(solution)/shard_map/pallas_call | solution.py:680
  158.9 1.6 %copy.20 = bf16[128,896]{1,0:T(8,128)(2,1)} copy(bf16[128,896]{1,0:T(8,128)(2,1)} %get-tuple-element.4) | data formatting | bytes 458752
  160.5 1.6 %copy.21 = bf16[128,896]{1,0:T(8,128)(2,1)} copy(bf16[128,896]{1,0:T(8,128)(2,1)} %get-tuple-element.5) | data formatting | bytes 458752

commit v2 on v1

--- a/solution.py
+++ b/solution.py
@@ -54,6 +54,7 @@
     qr,
     acc,
     row_max,
+    row_sum,
     part_send,
     part_recv,
     stat_send,
@@ -99,6 +100,7 @@
     weight_send,
     weight_recv,
     weight_local,
+    column,
 ):
     seq, head = lax.axis_index("seq"), lax.axis_index("head")
     y, z = lax.div(seq, 16), lax.rem(seq, 8)
@@ -118,6 +120,7 @@
     pair = dev(y, xh, z, 1 - xl, core)
     diagonal = dev(y, xh, z, 1 - xl, other)
     twin = dev(y, 1 - xh, z, xl, core)
+    cross = dev(y, 1 - xh, z, 1 - xl, core)
 
     def wrap(a, n):
         return lax.rem(a + n, n)
@@ -142,26 +145,16 @@
         partner,
         pair,
         diagonal,
+        cross,
     ):
         greet(device)
 
-    def greet_far(i, carry):
-        greet(far(lax.rem(my_j + i, 32)))
-        return carry
-
-    lax.fori_loop(1, 32, greet_far, 0)
-
-    @pl.when(core == 1)
-    def _():
-        greet(far(my_j))
-
     for j in range(4):
         qr[j * TOK : (j + 1) * TOK, :] = q_ref[:, j * HD : (j + 1) * HD]
-    kv[:, :, 256:384] = jnp.ones((32, TOK, HD), BF16)
     kv[my_kv, :, 0:128] = k_ref[...]
     kv[my_kv, :, 128:256] = v_ref[...]
-    gains[core, :, :] = jnp.broadcast_to(gain_ref[...].astype(F32), (8, QUARTER))
-    pl.semaphore_wait(barrier, 39 + core)
+    gains[core, :, :] = jnp.broadcast_to(gain_ref[...].astype(F32).reshape(1, QUARTER), (8, QUARTER))
+    pl.semaphore_wait(barrier, 9)
 
     def rcopy(src, dst, send, recv, device):
         return pltpu.make_async_remote_copy(
@@ -174,10 +167,10 @@
         )
 
     def part_a(b):
-        return kv.at[b, pl.ds(0, ROWS_A), pl.ds(0, 256)]
+        return kv.at[b, pl.ds(0, ROWS_A)]
 
     def part_b(b):
-        return kv.at[b, pl.ds(ROWS_A, TOK - ROWS_A), pl.ds(0, 256)]
+        return kv.at[b, pl.ds(ROWS_A, TOK - ROWS_A)]
 
     def send_a(zb, yb, y_, z_):
         b = zb * 4 + yb
@@ -239,8 +232,17 @@
         local.start()
         ffn_copies += [remote, local]
 
-    acc[...] = jnp.zeros((1024, 256), F32)
+    acc[...] = jnp.zeros((1024, HD), F32)
+    row_sum[...] = jnp.zeros((1024, HD), F32)
     row_max[...] = jnp.full((1024, HD), -1e30, F32)
+
+    eye = iota((TOK, TOK), 0) == iota((TOK, TOK), 1)
+
+    def to_row(column):
+        return jnp.sum(jnp.where(eye, column, 0.0), axis=0, keepdims=True)
+
+    def to_column(row):
+        return jnp.sum(jnp.where(eye, row, 0.0), axis=1, keepdims=True)
 
     lane = iota((1, 384), 1)
     main = lane < 256
@@ -248,13 +250,13 @@
     j_row = jnp.where(main, lax.shift_right_logical(lane, 3), lax.shift_right_logical(jnp.maximum(extra, 0), 1))
     s_row = jnp.where(main, lane & 7, 8 + (extra & 1))
     e_row = lax.shift_right_logical(j_row, 3) * 16 + far_h * 8 + (j_row & 7)
-    e_row = jnp.where(j_row < 32, e_row, -1)
+    e_row = jnp.where(j_row < 32, e_row, -1).astype(F32)
     named = jnp.zeros((TOK, 384), F32)
     weight = jnp.zeros((TOK, 384), F32)
     for k in range(4):
-        same = routes_ref[:, k : k + 1] == e_row
+        same = to_column(routes_ref[k : k + 1, :].astype(F32)) == e_row
         named = jnp.where(same, 1.0, named)
-        weight = jnp.where(same, weight_ref[:, k : k + 1], weight)
+        weight = jnp.where(same, to_column(weight_ref[k : k + 1, :]), weight)
     earlier = jnp.where(iota((TOK, TOK), 1) < iota((TOK, TOK), 0), 1.0, 0.0).astype(BF16)
     count = dot(earlier, named.astype(BF16))
     taken = jnp.where(count == s_row.astype(F32), named, 0.0)
@@ -270,29 +272,21 @@
         perm[which] = jnp.where((source == i) & (rem < 28), 1.0, 0.0).astype(BF16)
     rmat[...] = jnp.zeros((384, HALF), BF16)
 
-    eye = iota((TOK, TOK), 0) == iota((TOK, TOK), 1)
-
-    def to_row(column):
-        return jnp.sum(jnp.where(eye, column, 0.0), axis=0, keepdims=True)
-
-    def to_column(row):
-        return jnp.sum(jnp.where(eye, row, 0.0), axis=1, keepdims=True)
-
     def flash(zb, first, count):
         block = kv[pl.ds(zb * 4, 4)]
         keys = block[:, :, 0:128].reshape(512, HD)
-        values = block[:, :, 128:384].reshape(512, 256)
+        values = block[:, :, 128:256].reshape(512, HD)
 
         def tile(t, carry):
             rows = pl.ds(pl.multiple_of(first + t * 256, 256), 256)
             scores = dot_nt(qr[rows, :], keys)
             old = row_max[rows, :]
             new = jnp.maximum(old, jnp.max(scores, axis=1, keepdims=True))
-            p = jnp.exp2((scores - new[:, 0:1]) * SCALE2).astype(BF16)
+            p = jnp.exp2((scores - new[:, 0:1]) * SCALE2)
             fade = jnp.exp2((old - new) * SCALE2)
-            add = dot(p, values)
-            acc[rows, 0:128] = acc[rows, 0:128] * fade + add[:, 0:128]
-            acc[rows, 128:256] = acc[rows, 128:256] * fade + add[:, 128:256]
+            lanes = (p[:, 0:128] + p[:, 128:256]) + (p[:, 256:384] + p[:, 384:512])
+            row_sum[rows, :] = row_sum[rows, :] * fade + lanes
+            acc[rows, :] = acc[rows, :] * fade + dot(p.astype(BF16), values)
             row_max[rows, :] = new
             return carry
 
@@ -381,11 +375,15 @@
     for yb in range(4):
         wait_b(zf, yb)
 
+    @pl.when(core == 1)
+    def _():
+        pl.semaphore_signal(column, inc=1, device_id=cross, device_id_type=MESH)
+
     flash(zf, 512, 512)
     for j in range(4):
         rows = pl.ds(512 + j * TOK, TOK)
-        total = acc[rows, 128:256]
-        part_send[j * TOK : (j + 1) * TOK, :] = (acc[rows, 0:128] / total).astype(BF16)
+        total = jnp.sum(row_sum[rows, :], axis=1, keepdims=True)
+        part_send[j * TOK : (j + 1) * TOK, :] = (acc[rows, :] / total).astype(BF16)
         stat_send[j : j + 1, :] = to_row(row_max[rows, :] * SCALE2 + jnp.log2(total))
     stat_send[4:8, :] = jnp.zeros((4, TOK), F32)
     part_copy = rcopy(part_send, part_recv, misc_send.at[2], misc_recv.at[2], twin)
@@ -397,8 +395,8 @@
     stat_copy.wait_recv()
     for j in range(4):
         rows = slice(j * TOK, (j + 1) * TOK)
-        total = acc[rows, 128:256]
-        own = acc[rows, 0:128] / total
+        total = jnp.sum(row_sum[rows, :], axis=1, keepdims=True)
+        own = acc[rows, :] / total
         own_stat = row_max[rows, :] * SCALE2 + jnp.log2(total)
         their_stat = to_column(stat_recv[j : j + 1, :])
         own_share = 1.0 / (1.0 + jnp.exp2(their_stat - own_stat))
@@ -481,6 +479,10 @@
     def landing():
         return xbuf.at[xl, my_j]
 
+    @pl.when(core == 1)
+    def _():
+        pl.semaphore_wait(column, 1)
+
     @pl.when(core_zero)
     def _():
         pltpu.make_async_copy(send_buf.at[my_j], xbuf.at[xl, my_j], rd.at[my_j]).start()
@@ -539,8 +541,7 @@
         x = xmat[...]
         parts = []
         for c in range(2):
-            hidden = dot(x, gu[c])
-            gate, up = hidden[:, :HID], hidden[:, HID:]
+            gate, up = dot_nt(x, gu[c, 0:HID]), dot_nt(x, gu[c, HID : 2 * HID])
             parts.append((gate / (1.0 + jnp.exp(-gate)) * up).astype(BF16))
 
         def result(half, n):
@@ -648,8 +649,8 @@
     def drain(ref, sem):
         pltpu.make_async_copy(ref, ref, sem).wait()
 
-    drain(kv.at[pl.ds(0, 31), pl.ds(0, ROWS_A), pl.ds(0, 256)], sa)
-    drain(kv.at[pl.ds(0, 31), pl.ds(ROWS_A, TOK - ROWS_A), pl.ds(0, 256)], sb)
+    drain(kv.at[pl.ds(0, 31), pl.ds(0, ROWS_A)], sa)
+    drain(kv.at[pl.ds(0, 31), pl.ds(ROWS_A, TOK - ROWS_A)], sb)
     drain(xbuf.at[0], sp)
     for sem in (sd, sr):
 
@@ -686,9 +687,10 @@
         in_specs=[vmem, vmem, vmem, vmem, hbm, vmem, vmem, vmem, hbm, hbm],
         out_specs=(vmem, vmem),
         scratch_shapes=[
-            pltpu.VMEM((32, TOK, 384), BF16),
+            pltpu.VMEM((32, TOK, 256), BF16),
             pltpu.VMEM((1024, HD), BF16),
-            pltpu.VMEM((1024, 256), F32),
+            pltpu.VMEM((1024, HD), F32),
+            pltpu.VMEM((1024, HD), F32),
             pltpu.VMEM((1024, HD), F32),
             pltpu.VMEM((512, HD), BF16),
             pltpu.VMEM((512, HD), BF16),
@@ -708,7 +710,7 @@
             pltpu.VMEM((32, SLOT_ROWS, 128), BF16),
             pltpu.VMEM((2, 32, SLOT_ROWS, 128), BF16),
             pltpu.VMEM((GROUP_ROWS, D), BF16),
-            pltpu.VMEM((2, D, 2 * HID), BF16),
+            pltpu.VMEM((2, 2 * HID, D), BF16),
             pltpu.VMEM((2, HID, D), BF16),
             pltpu.VMEM((GROUPS, GROUP_ROWS, HALF), BF16),
             pltpu.VMEM((GROUPS, GROUP_ROWS, HALF), BF16),
@@ -735,6 +737,7 @@
             dma((4,)),
             dma((4,)),
             dma((4,)),
+            pltpu.SemaphoreType.REGULAR,
         ],
         compiler_params=pltpu.CompilerParams(
             collective_id=0,
@@ -750,10 +753,10 @@
         value_heads,
         residual,
         out_proj,
-        norm_gain.reshape(1, QUARTER),
-        routes,
-        combine_weight,
-        gate_up.reshape(D, 2 * HID),
+        norm_gain,
+        routes.T,
+        combine_weight.T,
+        gate_up.reshape(D, 2 * HID).T,
         down_proj.reshape(HID, D),
     )
 

time: 163 us -> 144 us (0.88)
  local copies, waits for them, and re-layouts: 14.6 us -> 3.29 us
  Pallas kernels: 147 us -> 140 us
    reshape x2 -> x0, local copies, waits for them, and re-layouts: 8.49 us -> none  [the longest x1 7.22 us: body(): gate_up.reshape(D, 2 * HID)]
    pallas_call x1, Pallas kernels: 147 us -> 140 us  [body(): pl.pallas_call(kernel, out_shape=(jax.ShapeDtypeStruct((TOK, QUARTER), BF...]
    unnamed x4 -> x2, local copies, waits for them, and re-layouts: 6.12 us -> 3.29 us
where the time goes in v2:
time: 144 us
  Pallas kernels  140 us (97%)
  local copies, waits for them, and re-layouts  3.29 us (2%)
    pallas_call x1, Pallas kernels, body(): pl.pallas_call(kernel, out_shape=(jax.ShapeDtypeStruct((TOK, QUARTER), BF...  140 us
    unnamed x2, local copies, waits for them, and re-layouts  3.29 us

profile of v2, /device:TPU:1, one launch (start us, length us, event | category | flops | bytes accessed | tf_op | source)
XLA Modules:
  0.0 144.1 jit_solution(10818191319071552919)
XLA Ops:
  0.6 140.1 %shard_map.113 = (bf16[128,896]{1,0:T(8,128)(2,1)}, bf16[128,896]{1,0:T(8,128)(2,1)}) custom-call(bf16[128,512]{1,0:T(8,128)(2,1)} %q_ref.1, bf16[128,128]{1,0:T(8,128)(2,1)} %k_ref.1, bf16[128,128]{1,0:T(8,128)(2,1)} %v_ref.1, bf16[128,896]{1,0:T(8,128)(2,1)} %residual_ref.1, bf16[512,3584]{1,0:T(8,128)(2,1)} %out_proj_ref.1, bf16[896]{0:T(1024)(128)(2,1)} %gain_ref.1, ...), custom_call_target="tpu_custom_call" | custom-call | flops 8000000000 | bytes 20000000 | tf_op jit(solution)/shard_map/pallas_call | solution.py:681
  140.8 1.6 %copy.14 = bf16[128,896]{1,0:T(8,128)(2,1)} copy(bf16[128,896]{1,0:T(8,128)(2,1)} %get-tuple-element.4) | data formatting | bytes 458752
  142.4 1.6 %copy.15 = bf16[128,896]{1,0:T(8,128)(2,1)} copy(bf16[128,896]{1,0:T(8,128)(2,1)} %get-tuple-element.5) | data formatting | bytes 458752

commit v3 on v2

--- a/solution.py
+++ b/solution.py
@@ -13,7 +13,6 @@
 QUARTER = 896
 HALF = 1792
 HID = 320
-ROWS_A = 80
 SLOT_ROWS = 144
 GROUP = 8
 GROUPS = 4
@@ -107,7 +106,7 @@
     xh = lax.rem(lax.div(seq, 8), 2)
     xl, core = lax.div(head, 2), lax.rem(head, 2)
     other = 1 - core
-    z_even, y_even, core_zero = lax.rem(z, 2) == 0, lax.rem(y, 2) == 0, core == 0
+    core_zero = core == 0
     my_kv = z * 4 + y
     my_j = y * 8 + z
     far_h, far_l = (xh + core) % 2, (xl + core) % 2
@@ -139,6 +138,7 @@
     for device in (
         dev(yp, xh, z, xl, core),
         dev(ym, xh, z, xl, core),
+        dev(y2, xh, z, xl, core),
         dev(y, xh, zp, xl, core),
         dev(y, xh, zm, xl, core),
         twin,
@@ -154,7 +154,7 @@
     kv[my_kv, :, 0:128] = k_ref[...]
     kv[my_kv, :, 128:256] = v_ref[...]
     gains[core, :, :] = jnp.broadcast_to(gain_ref[...].astype(F32).reshape(1, QUARTER), (8, QUARTER))
-    pl.semaphore_wait(barrier, 9)
+    pl.semaphore_wait(barrier, 10)
 
     def rcopy(src, dst, send, recv, device):
         return pltpu.make_async_remote_copy(
@@ -166,42 +166,37 @@
             device_id_type=MESH,
         )
 
-    def part_a(b):
-        return kv.at[b, pl.ds(0, ROWS_A)]
-
-    def part_b(b):
-        return kv.at[b, pl.ds(ROWS_A, TOK - ROWS_A)]
-
-    def send_a(zb, yb, y_, z_):
-        b = zb * 4 + yb
-        rcopy(part_a(b), part_a(b), sa, ra.at[b], dev(y_, xh, z_, xl, core)).start()
-
-    def send_b(zb, yb, y_, z_):
-        b = zb * 4 + yb
-        rcopy(part_b(b), part_b(b), sb, rb.at[b], dev(y_, xh, z_, xl, core)).start()
-
-    def wait_a(zb, yb):
-        b = zb * 4 + yb
-        pltpu.make_async_copy(part_a(b), part_a(b), ra.at[b]).wait()
-
-    def wait_b(zb, yb):
-        b = zb * 4 + yb
-        pltpu.make_async_copy(part_b(b), part_b(b), rb.at[b]).wait()
-
-    send_a(z, y, y, zp)
-    send_a(z, y, y, zm)
-    send_b(z, y, yp, z)
-    send_b(z, y, ym, z)
-    send_a(z, y, yp, z)
-    send_a(z, y, ym, z)
-    send_b(z, y, y, zp)
-    send_b(z, y, y, zm)
+    def y_block(yb):
+        return kv.at[z * 4 + yb]
+
+    def bundle(zb, h):
+        return kv.at[pl.ds(zb * 4 + h * 2, 2)]
+
+    def send_bundle(zb, h, to):
+        part = bundle(zb, h)
+        rcopy(part, part, sa, ra.at[zb * 2 + h], dev(y, xh, to, xl, core)).start()
+
+    def wait_bundle(zb, h):
+        part = bundle(zb, h)
+        pltpu.make_async_copy(part, part, ra.at[zb * 2 + h]).wait()
+
+    near = y + 1 - 2 * lax.rem(y, 2)
+    others = (near, lax.rem(near + 2, 4), y2)
+    for yb in others:
+        rcopy(y_block(y), y_block(y), sb, rb.at[y], dev(yb, xh, z, xl, core)).start()
     q_copy = rcopy(
         qr.at[pl.ds(0, 512)], qr.at[pl.ds(512, 512)], misc_send.at[0], misc_recv.at[0], twin
     )
     q_copy.start()
     gain_copy = rcopy(gains.at[core], gains.at[core], misc_send.at[1], misc_recv.at[1], partner)
     gain_copy.start()
+
+    h_near = lax.div(y, 2)
+    for h, sources in ((h_near, others[0:1]), (1 - h_near, others[1:3])):
+        for yb in sources:
+            pltpu.make_async_copy(y_block(yb), y_block(yb), rb.at[yb]).wait()
+        send_bundle(z, h, zp)
+        send_bundle(z, h, zm)
 
     wo_copies = []
     for hf in range(2):
@@ -292,88 +287,31 @@
 
         lax.fori_loop(0, count // 256, tile, 0)
 
-    def y_stage(zb):
-        even = lax.rem(zb, 2) == 0
-        wait_a(zb, ym)
-
-        @pl.when(even)
-        def _():
-            send_a(zb, ym, yp, z)
-
-        wait_a(zb, yp)
-
-        @pl.when(jnp.logical_not(even))
-        def _():
-            send_a(zb, yp, ym, z)
-
-    for yb, forward, to in ((ym, z_even, yp), (yp, jnp.logical_not(z_even), ym)):
-        wait_b(z, yb)
-        send_b(z, yb, y, zp)
-        send_b(z, yb, y, zm)
-
-        @pl.when(forward)
-        def _():
-            send_b(z, yb, to, z)
-
-    y_stage(z)
-    wait_b(z, y2)
-    send_b(z, y2, y, zp)
-    send_b(z, y2, y, zm)
-
-    def z_stage(d):
-        for zb, to, parity in ((wrap(z - d, 8), zp, 0), (wrap(z + d, 8), zm, 1)):
-            wait_a(zb, y)
-            goes = (d < 3) | ((d == 3) & (lax.rem(y, 2) == parity))
-
-            @pl.when(goes)
+    def step(d, carry):
+        ahead, behind = wrap(z - d, 8), wrap(z + d, 8)
+        for h in (h_near, 1 - h_near):
+            wait_bundle(ahead, h)
+
+            @pl.when((d < 3) | (h == 0))
             def _():
-                send_a(zb, y, y, to)
-
-            send_a(zb, y, yp, z)
-            send_a(zb, y, ym, z)
-
-            def each(yb, carry):
-                wait_b(zb, yb)
-
-                @pl.when((d < 3) | ((d == 3) & (lax.rem(yb, 2) == parity)))
-                def _():
-                    send_b(zb, yb, y, to)
-
-                return carry
-
-            lax.fori_loop(0, 4, each, 0)
-
-    def step(d, carry):
-        z_stage(d)
-
-        @pl.when(d == 1)
-        def _():
-            q_copy.wait_recv()
-            wait_a(z, y2)
-            flash(z, 0, 1024)
-
-        @pl.when(d > 1)
-        def _():
-            for zb in (wrap(z - d + 1, 8), wrap(z + d - 1, 8)):
-                wait_a(zb, y2)
-                flash(zb, 0, 1024)
-
-        y_stage(wrap(z - d, 8))
-        y_stage(wrap(z + d, 8))
+                send_bundle(ahead, h, zp)
+
+            wait_bundle(behind, h)
+
+            @pl.when((d < 3) | (h == 1))
+            def _():
+                send_bundle(behind, h, zm)
+
+        flash(ahead, 0, 1024)
+        flash(behind, 0, 1024)
         return carry
 
+    q_copy.wait_recv()
+    flash(z, 0, 1024)
     lax.fori_loop(1, 4, step, 0)
     zf = wrap(z + 4, 8)
-    wait_a(zf, y)
-    send_a(zf, y, yp, z)
-    send_a(zf, y, ym, z)
-    for zb in (wrap(z - 3, 8), wrap(z + 3, 8)):
-        wait_a(zb, y2)
-        flash(zb, 0, 1024)
-    y_stage(zf)
-    wait_a(zf, y2)
-    for yb in range(4):
-        wait_b(zf, yb)
+    for h in range(2):
+        wait_bundle(zf, h)
 
     @pl.when(core == 1)
     def _():
@@ -649,8 +587,8 @@
     def drain(ref, sem):
         pltpu.make_async_copy(ref, ref, sem).wait()
 
-    drain(kv.at[pl.ds(0, 31), pl.ds(0, ROWS_A)], sa)
-    drain(kv.at[pl.ds(0, 31), pl.ds(ROWS_A, TOK - ROWS_A)], sb)
+    drain(kv.at[pl.ds(0, 28)], sa)
+    drain(kv.at[pl.ds(0, 3)], sb)
     drain(xbuf.at[0], sp)
     for sem in (sd, sr):
 
@@ -720,8 +658,8 @@
             pltpu.VMEM((384, HALF), BF16),
             pltpu.VMEM((TOK, QUARTER), BF16),
             pltpu.VMEM((TOK, QUARTER), BF16),
-            dma((32,)),
-            dma((32,)),
+            dma((16,)),
+            dma((4,)),
             dma((32,)),
             dma((32,)),
             dma((GROUPS,)),

time: 144 us -> 134 us (0.931)
  Pallas kernels: 140 us -> 130 us
    pallas_call x1, Pallas kernels: 140 us -> 130 us  [body(): pl.pallas_call(kernel, out_shape=(jax.ShapeDtypeStruct((TOK, QUARTER), BF...]
where the time goes in v3:
time: 134 us
  Pallas kernels  130 us (97%)
  local copies, waits for them, and re-layouts  3.29 us (2%)
    pallas_call x1, Pallas kernels, body(): pl.pallas_call(kernel, out_shape=(jax.ShapeDtypeStruct((TOK, QUARTER), BF...  130 us
    unnamed x2, local copies, waits for them, and re-layouts  3.29 us

profile of v3, /device:TPU:1, one launch (start us, length us, event | category | flops | bytes accessed | tf_op | source)
XLA Modules:
  0.0 133.6 jit_solution(13091805601942807899)
XLA Ops:
  0.6 129.7 %shard_map.113 = (bf16[128,896]{1,0:T(8,128)(2,1)}, bf16[128,896]{1,0:T(8,128)(2,1)}) custom-call(bf16[128,512]{1,0:T(8,128)(2,1)} %q_ref.1, bf16[128,128]{1,0:T(8,128)(2,1)} %k_ref.1, bf16[128,128]{1,0:T(8,128)(2,1)} %v_ref.1, bf16[128,896]{1,0:T(8,128)(2,1)} %residual_ref.1, bf16[512,3584]{1,0:T(8,128)(2,1)} %out_proj_ref.1, bf16[896]{0:T(1024)(128)(2,1)} %gain_ref.1, ...), custom_call_target="tpu_custom_call" | custom-call | flops 8000000000 | bytes 20000000 | tf_op jit(solution)/shard_map/pallas_call | solution.py:619
  130.3 1.6 %copy.14 = bf16[128,896]{1,0:T(8,128)(2,1)} copy(bf16[128,896]{1,0:T(8,128)(2,1)} %get-tuple-element.4) | data formatting | bytes 458752
  132.0 1.6 %copy.15 = bf16[128,896]{1,0:T(8,128)(2,1)} copy(bf16[128,896]{1,0:T(8,128)(2,1)} %get-tuple-element.5) | data formatting | bytes 458752

commit v4 on v3

--- a/solution.py
+++ b/solution.py
@@ -47,8 +47,7 @@
     weight_ref,
     gate_up_ref,
     down_ref,
-    mid_ref,
-    out_ref,
+    both_ref,
     kv,
     qr,
     acc,
@@ -365,7 +364,7 @@
         mid_half.at[core], mid_half.at[core], misc_send.at[6], misc_recv.at[6], partner
     )
     mid_copy.start()
-    mid_ref[...] = middle
+    both_ref[0:TOK, :] = middle
     mid_float = middle.astype(F32)
     squares[head] = jnp.broadcast_to(
         to_row(jnp.sum(mid_float * mid_float, axis=1, keepdims=True)), (8, TOK)
@@ -534,28 +533,35 @@
         def _():
             forward(g + 1)
 
+        @pl.when((g > 0) & (g < GROUPS - 1))
+        def _():
+            give_back(g - 1)
+
         gather_rows(g)
         experts(g)
-
-        @pl.when(g > 0)
-        def _():
-            give_back(g - 1)
-
         return carry
 
     lax.fori_loop(0, GROUPS, turn, 0)
-    give_back(GROUPS - 1)
-
-    def await_return(i, carry):
-        j = lax.rem(my_j + i, 32)
-        pltpu.make_async_copy(ret.at[j], ret.at[j], rr.at[j]).wait()
+
+    def last(g, carry):
+        give_back(g)
         return carry
 
-    lax.fori_loop(0, 32, await_return, 0)
-    for c in range(0, 14, 2):
-        both = ret[:, c * 8 : c * 8 + 16, :].astype(F32)
-        for n in range(2):
-            rmat[0:256, lane_block(c + n)] = both[:, 8 * n : 8 * n + 8].reshape(256, 128).astype(BF16)
+    lax.fori_loop(GROUPS - 2, GROUPS, last, 0)
+
+    def take_back(n, carry):
+        p = lax.rem(lax.div(my_j, 2) + n, 16)
+        for m in range(2):
+            j = p * 2 + m
+            pltpu.make_async_copy(ret.at[j], ret.at[j], rr.at[j]).wait()
+        both = [ret[p * 2 + m, 0:112, :].astype(F32).reshape(14, 8, 128) for m in range(2)]
+        taken = jnp.concatenate(both, axis=1).astype(BF16)
+        rows = pl.ds(pl.multiple_of(p * 16, 16), 16)
+        for c in range(14):
+            rmat[rows, lane_block(c)] = taken[c]
+        return carry
+
+    lax.fori_loop(1, 17, take_back, 0)
     for g in range(4):
         stack = ret[8 * g : 8 * g + 8, 112:144, :].reshape(256, 128)
         rows = dot(perm[1], stack).astype(BF16)
@@ -572,7 +578,7 @@
     comb_copy.start()
     own = combined(core)
     comb_copy.wait_recv()
-    out_ref[...] = (own + comb_recv[...].astype(F32)).astype(BF16)
+    both_ref[TOK : 2 * TOK, :] = (own + comb_recv[...].astype(F32)).astype(BF16)
 
     for copy in (
         [q_copy, gain_copy, part_copy, stat_copy, att_copy, rs_copy, mid_copy, comb_copy]
@@ -616,14 +622,11 @@
     vmem = pl.BlockSpec(memory_space=pltpu.VMEM)
     hbm = pl.BlockSpec(memory_space=pl.ANY)
     dma = pltpu.SemaphoreType.DMA
-    return pl.pallas_call(
+    both = pl.pallas_call(
         kernel,
-        out_shape=(
-            jax.ShapeDtypeStruct((TOK, QUARTER), BF16),
-            jax.ShapeDtypeStruct((TOK, QUARTER), BF16),
-        ),
+        out_shape=jax.ShapeDtypeStruct((2 * TOK, QUARTER), BF16),
         in_specs=[vmem, vmem, vmem, vmem, hbm, vmem, vmem, vmem, hbm, hbm],
-        out_specs=(vmem, vmem),
+        out_specs=vmem,
         scratch_shapes=[
             pltpu.VMEM((32, TOK, 256), BF16),
             pltpu.VMEM((1024, HD), BF16),
@@ -697,6 +700,7 @@
         gate_up.reshape(D, 2 * HID).T,
         down_proj.reshape(HID, D),
     )
+    return both[0:TOK], both[TOK : 2 * TOK]
 
 
 def solution(mesh):

time: 134 us -> 132 us (0.985)
  local copies, waits for them, and re-layouts: 3.29 us -> 1.85 us
    unnamed x2 -> x0, local copies, waits for them, and re-layouts: 3.29 us -> none
    slice x0 -> x1, local copies, waits for them, and re-layouts: none -> 1.85 us  [body(): return (both[0:TOK], both[TOK:2 * TOK])]
where the time goes in v4:
time: 132 us
  Pallas kernels  130 us (98%)
  local copies, waits for them, and re-layouts  1.85 us (1%)
    pallas_call x1, Pallas kernels, body(): pl.pallas_call(kernel, out_shape=jax.ShapeDtypeStruct((2 * TOK, QUARTER),...  130 us

profile of v4, /device:TPU:1, one launch (start us, length us, event | category | flops | bytes accessed | tf_op | source)
XLA Modules:
  0.0 132.1 jit_solution(10987382419395868952)
XLA Ops:
  0.6 129.6 %shard_map.113 = bf16[256,896]{1,0:T(8,128)(2,1)} custom-call(bf16[128,512]{1,0:T(8,128)(2,1)} %q_ref.1, bf16[128,128]{1,0:T(8,128)(2,1)} %k_ref.1, bf16[128,128]{1,0:T(8,128)(2,1)} %v_ref.1, bf16[128,896]{1,0:T(8,128)(2,1)} %residual_ref.1, bf16[512,3584]{1,0:T(8,128)(2,1)} %out_proj_ref.1, bf16[896]{0:T(1024)(128)(2,1)} %gain_ref.1, s32[4,128]{1,0:T(4,128)} %bitcast.8, ...), custom_call_target="tpu_custom_call" | custom-call | flops 8000000000 | bytes 20000000 | tf_op jit(solution)/shard_map/pallas_call | solution.py:625
  130.2 1.9 %fusion = (bf16[128,896]{1,0:T(8,128)(2,1)}, bf16[128,896]{1,0:T(8,128)(2,1)}) fusion(bf16[256,896]{1,0:T(8,128)(2,1)} %shard_map.113), kind=kLoop, calls=%fused_computation | loop fusion | bytes 917504 | tf_op jit(solution)/shard_map/slice | solution.py:703
